TPU v7x, 32 devices: a whole 2x2x4 slice. The times are simulated.
32 devices in a mesh: robot: 2 (over x), xy: 4 (over z), yz: 4 (over y, core).
Axes of the slice: x: 2, y: 2, z: 4, core: 2. Of those that a mesh axis runs over, the one named last changes fastest.
Arguments:
- seed_cost: bfloat16 [4, 64, 512, 512], P('robot', None, 'xy', 'yz'), may hold values from 0 to 9
- occupied: int32 [64, 512, 512], P(None, 'xy', 'yz'), may hold values from 0 to 1, as said below
- unknown: int32 [64, 512, 512], P(None, 'xy', 'yz'), may hold values from 0 to 1, as said below
Outputs:
- signed: float32 [64, 512, 512], P(('robot', 'xy'), 'yz')
Inputs may be any that keep to these rules, and one draw needn't show every extreme that they name: At least one cell is occupied. At least one cell is neither occupied nor unknown.
All inputs are finite; a program needn't handle non-finite values.
Results may differ from a plain program's by a relative error of at most 0.0003.
Values may be sent and summed in bfloat16 or wider, within the bound.
A program may use at most 64 MiB of HBM per device.

v0:
```python
import jax
import jax.numpy as jnp
from jax import lax
from jax.sharding import PartitionSpec as P

penalty = 1048576.0
voxel_size = 0.2


def lower_envelope(values, along):
    extent = values.shape[along]
    block_size = min(extent, 128)
    places = jnp.arange(extent, dtype=jnp.float32)
    pieces = []
    for offset in range(0, extent, block_size):
        target = places[offset : offset + block_size]
        table = (places[:, None] - target[None, :]) ** 2
        layout = [1] * (values.ndim + 1)
        layout[along] = extent
        layout[along + 1] = block_size
        summed = jnp.expand_dims(values, along + 1) + table.reshape(layout)
        pieces.append(jnp.min(summed, axis=along))
    return jnp.concatenate(pieces, axis=along)


def seed_fields(lowest_cost, occupied, unknown):
    merged_cost = lowest_cost.astype(jnp.float32)
    outside = jnp.where(occupied == 1, merged_cost, merged_cost + penalty)
    inside = jnp.where((occupied == 1) | (unknown == 1), merged_cost + penalty, merged_cost)
    return jnp.stack([outside, inside])


def along_rows(blocks):
    return lower_envelope(blocks, 2)


def along_columns(blocks):
    return lower_envelope(blocks, 3)


def body(seed_cost, occupied, unknown):
    local_lowest = jnp.min(seed_cost, axis=0)
    merged = lax.pmin(local_lowest, "robot")
    fields = lower_envelope(seed_fields(merged, occupied, unknown), 1)
    half_depth = fields.shape[1] // lax.axis_size("robot")
    own_half = lax.dynamic_slice_in_dim(fields, lax.axis_index("robot") * half_depth, half_depth, 1)
    crossed = along_rows(lax.all_to_all(own_half, "xy", split_axis=1, concat_axis=2, tiled=True))
    settled = along_columns(lax.all_to_all(crossed, "yz", split_axis=2, concat_axis=3, tiled=True))
    return voxel_size * (jnp.sqrt(settled[0]) - jnp.sqrt(settled[1]))


def solution(mesh):
    in_specs = (P("robot", None, "xy", "yz"), P(None, "xy", "yz"), P(None, "xy", "yz"))
    out_specs = P(("robot", "xy"), "yz", None)
    return jax.shard_map(body, mesh=mesh, in_specs=in_specs, out_specs=out_specs, check_vma=False)
```

profile of v0, /device:TPU:0, one launch (start us, length us, event | category | flops | bytes accessed | tf_op | source)
XLA Modules:
  0.0 1384.9 jit_solution(17854108510850008779)
XLA Ops:
  6.5 0.0 all-reduce.2.cloned.1.call-start
  6.5 5.1 reduce_min.90
  11.6 0.0 all-reduce.2.cloned.1.call-update
  11.7 65.7 %all-reduce.2.cloned.1.call-done = bf16[64,128,128]{2,1,0:T(8,128)(2,1)} async-done(((bf16[64,128,128]{2,1,0:T(8,128)(2,1)}), bf16[64,128,128]{2,1,0:T(8,128)(2,1)}) %all-reduce.2.cloned.1.call-update) | async-done | bytes 2097168 | tf_op jit(solution)/shard_map/pmin | solution.py:43
  77.4 0.0 copy-start
  77.4 0.0 copy-start.1
  77.4 4.0 fusion
  81.4 0.0 copy-done
  81.4 0.7 copy-done.1
  82.1 1.1 fusion.1
  83.2 3.8 pad_maximum_fusion
  87.0 162.6 %add_reduce_fusion.8 = f32[2,64,128,128]{3,2,1,0:T(8,128)} fusion(f32[64,64]{1,0:T(8,128)S(1)} %subtract_multiply_fusion.4, f32[2,64,128,128]{3,2,1,0:T(8,128)} %pad_maximum_fusion), kind=kLoop, calls=%fused_computation.8 | loop fusion | flops 266338304 | bytes 16793600 | tf_op jit(solution)/shard_map/reduce_min | solution.py:22
  249.6 2.5 constant_dynamic-slice_fusion
  252.1 2.2 copy.13
  254.3 5.0 all-to-all-start
  259.5 0.8 subtract_multiply_fusion
  260.3 0.9 subtract_multiply_fusion.2
  261.2 91.4 %all-to-all-done = f32[2,32,128,128]{3,2,0,1:T(8,128)} async-done(((f32[2,32,128,128]{3,2,0,1:T(8,128)}), f32[2,32,128,128]{3,2,0,1:T(8,128)}, u32[]{:S(2)}, u32[]{:S(2)}) %all-to-all-start) | async-done | bytes 4194336 | tf_op jit(solution)/shard_map/all_to_all | solution.py:47
  352.7 4.7 copy.15
  357.3 305.2 %add_reduce_fusion.7 = (f32[2,8,128,128]{3,2,1,0:T(8,128)S(1)}, f32[2,8,128,128]{3,2,1,0:T(8,128)S(1)}, f32[2,8,128,128]{3,2,1,0:T(8,128)S(1)}, f32[2,8,128,128]{3,2,1,0:T(8,128)}) fusion(f32[512,128]{1,0:T(8,128)} %get-tuple-element.18, f32[2,8,512,128]{3,2,1,0:T(8,128)} %bitcast.14, f32[512,128]{1,0:T(8,128)} %get-tuple-element.17, ...), kind=kLoop, calls=%fused_computation.7 | loop fusion | flops 1072693248 | bytes 9437184 | tf_op jit(solution)/shard_map/reduce_min | solution.py:22
  662.6 1.5 pad_maximum_fusion.1
  664.1 2.4 copy.16
  666.5 51.6 %all_to_all.30 = f32[2,8,512,128]{3,1,0,2:T(8,128)} all-to-all(f32[2,8,512,128]{3,1,0,2:T(8,128)S(1)} %copy.16), channel_id=1, replica_groups=mesh['robot'=2,'xy'=4,'yz'=4] {'yz'}, dimensions={2} | all-to-all | bytes 8388608 | tf_op jit(solution)/shard_map/all_to_all | solution.py:48
  718.1 5.3 copy.18
  723.4 0.0 copy-start.2
  723.4 0.0 copy-start.3
  723.4 0.0 copy-start.4
  723.4 5.5 copy.19
  728.9 0.0 copy-done.2
  728.9 0.0 copy-done.3
  728.9 0.0 copy-done.4
  728.9 646.4 %add_reduce_fusion.3 = (f32[2,8,128,128]{3,2,1,0:T(8,128)S(1)}, f32[2,8,128,128]{3,2,1,0:T(8,128)S(1)}, f32[2,8,128,128]{3,2,1,0:T(8,128)S(1)}, f32[2,8,128,128]{3,2,1,0:T(8,128)S(1)}) fusion(f32[512,128]{1,0:T(8,128)S(1)} %copy-done.4, f32[2,8,128,512]{3,2,1,0:T(8,128)} %copy.19, f32[512,128]{1,0:T(8,128)S(1)} %copy-done.3, f32[512,128]{1,0:T(8,128)S(1)} %copy-done.2, ...), kind=kLoop, calls=%fused_computation.3 | loop fusion | flops 1072693248 | bytes 9437184 | tf_op jit(solution)/shard_map/reduce_min | solution.py:22
  1375.3 0.3 pad_maximum_fusion.2
  1375.7 2.4 fusion.4
  (9 shorter events, 0.1 us)
Async XLA Ops:
  6.5 70.9 %all-reduce.2.cloned.1.call-start = ((), (), s32[]{:S(2)}) async-start(), calls=%async_computation.2 | async-start | bytes 4194304 | tf_op jit(solution)/shard_map/pmin | solution.py:43
  77.4 4.0 copy-start
  77.4 4.7 copy-start.1
  254.3 98.3 %all-to-all-start = ((f32[2,32,128,128]{3,2,0,1:T(8,128)}), f32[2,32,128,128]{3,2,0,1:T(8,128)}, u32[]{:S(2)}, u32[]{:S(2)}) async-start(f32[2,32,128,128]{3,2,0,1:T(8,128)} %copy.13), calls=%async_computation | async-start | bytes 8388608 | tf_op jit(solution)/shard_map/all_to_all | solution.py:47
  723.4 5.5 copy-start.2
  723.4 5.5 copy-start.3
  723.4 5.5 copy-start.4
Sparse Core Ops, SparseCore 0:
  11.8 65.6 all-reduce.1
where the time goes:
time: 1390 us; the launch traced here: 1380 us
  other arithmetic  1130 us (81%)
  waiting for transfers between devices  157 us (11%)
  blocking collectives  51.6 us (4%)
  local copies, waits for them, and re-layouts  23.2 us (2%)
    reduce_min x3, other arithmetic, lower_envelope(): pieces.append(jnp.min(summed, axis=along))  1110 us
    all_to_all x1, waiting for transfers between devices, body(): lax.all_to_all(own_half, 'xy', split_axis=1, concat_axis=2, tiled=True)  91.4 us
    pmin x1, waiting for transfers between devices, body(): merged = lax.pmin(local_lowest, 'robot')  65.7 us
    all_to_all x1, blocking collectives, body(): lax.all_to_all(crossed, 'yz', split_axis=2, concat_axis=3, tiled=True)  51.6 us
  transfers between devices with their start and end apart: 2, of which 2 were waited for; matrix products, arithmetic and copies ran while one was open for 0% of the time, Pallas kernels for 0%

commit v1 on v0

--- a/solution.py
+++ b/solution.py
@@ -1,10 +1,21 @@
+import functools
+import math
+
 import jax
 import jax.numpy as jnp
 from jax import lax
+from jax.experimental import pallas as pl
+from jax.experimental.pallas import tpu as pltpu
 from jax.sharding import PartitionSpec as P
 
 penalty = 1048576.0
 voxel_size = 0.2
+largest_cost = 9.0
+sharpness = 20.0
+codes = 65535.0
+span = math.log(1.0 + sharpness * (penalty + 1024.0))
+block = 16
+far_away = 4194304.0
 
 
 def lower_envelope(values, along):
@@ -30,23 +41,293 @@
     return jnp.stack([outside, inside])
 
 
-def along_rows(blocks):
-    return lower_envelope(blocks, 2)
-
-
-def along_columns(blocks):
-    return lower_envelope(blocks, 3)
-
-
-def body(seed_cost, occupied, unknown):
+def plain_body(seed_cost, occupied, unknown):
     local_lowest = jnp.min(seed_cost, axis=0)
     merged = lax.pmin(local_lowest, "robot")
     fields = lower_envelope(seed_fields(merged, occupied, unknown), 1)
     half_depth = fields.shape[1] // lax.axis_size("robot")
     own_half = lax.dynamic_slice_in_dim(fields, lax.axis_index("robot") * half_depth, half_depth, 1)
-    crossed = along_rows(lax.all_to_all(own_half, "xy", split_axis=1, concat_axis=2, tiled=True))
-    settled = along_columns(lax.all_to_all(crossed, "yz", split_axis=2, concat_axis=3, tiled=True))
+    crossed = lower_envelope(lax.all_to_all(own_half, "xy", split_axis=1, concat_axis=2, tiled=True), 2)
+    settled = lower_envelope(lax.all_to_all(crossed, "yz", split_axis=2, concat_axis=3, tiled=True), 3)
     return voxel_size * (jnp.sqrt(settled[0]) - jnp.sqrt(settled[1]))
+
+
+def encode(field):
+    scaled = jnp.log(1.0 + sharpness * field) * (codes / span) + 0.5
+    return (jnp.minimum(scaled, codes).astype(jnp.int32) - 32768).astype(jnp.int16)
+
+
+def decode(code):
+    scaled = (code.astype(jnp.int32) + 32768).astype(jnp.float32)
+    return (jnp.exp(scaled * (span / codes)) - 1.0) * (1.0 / sharpness)
+
+
+def depth_kernel(place_ref, cost_ref, other_ref, occupied_ref, unknown_ref, out_ref, in_ref, g_ref, h_ref):
+    depth = other_ref.shape[0]
+    rows, lanes = other_ref.shape[1:]
+    reach = math.isqrt(int(largest_cost)) + 1
+    wall = jnp.full((rows, lanes), far_away, jnp.float32)
+    for field in range(2):
+        for pad in range(reach):
+            g_ref[field, pad] = wall
+            g_ref[field, depth + reach + pad] = wall
+
+    def seeds(z, carry):
+        merged = jnp.minimum(jnp.minimum(cost_ref[0, z], cost_ref[1, z]), other_ref[z]).astype(jnp.float32)
+        occupied = occupied_ref[z] == 1
+        blocked = occupied | (unknown_ref[z] == 1)
+        fields = (jnp.where(occupied, merged, merged + penalty), jnp.where(blocked, merged + penalty, merged))
+        after = []
+        for field, (cost, away) in zip(range(2), carry):
+            value = fields[field]
+            g_ref[field, z + reach] = value
+            seed = value < penalty
+            cost = jnp.where(seed, value, cost)
+            away = jnp.where(seed, 0.0, away + 1.0)
+            h_ref[field, z] = cost + away * away
+            after.append((cost, away))
+        return tuple(after)
+
+    nothing = jnp.zeros((rows, lanes), jnp.float32)
+    lax.fori_loop(0, depth, seeds, ((wall, nothing), (wall, nothing)), unroll=4)
+
+    def settle(step, carry):
+        z = depth - 1 - step
+        after = []
+        for field, (cost, away) in zip(range(2), carry):
+            value = g_ref[field, z + reach]
+            seed = value < penalty
+            cost = jnp.where(seed, value, cost)
+            away = jnp.where(seed, 0.0, away + 1.0)
+            best = jnp.minimum(jnp.minimum(h_ref[field, z], cost + away * away), value)
+            for apart in range(1, reach + 1):
+                pair = jnp.minimum(g_ref[field, z + reach - apart], g_ref[field, z + reach + apart])
+                best = jnp.minimum(best, pair + float(apart * apart))
+            (out_ref, in_ref)[field][z] = encode(best)
+            after.append((cost, away))
+        return tuple(after)
+
+    lax.fori_loop(0, depth, settle, ((wall, nothing), (wall, nothing)), unroll=4)
+
+
+def depth_pass(seed_cost, other, occupied, unknown, half):
+    robots, depth, _, lanes = seed_cost.shape
+    rows = 16
+    steps = half // rows
+    reach = math.isqrt(int(largest_cost)) + 1
+    place = (lax.axis_index("robot") * steps).astype(jnp.int32).reshape(1)
+    shape = jax.ShapeDtypeStruct((depth, half, lanes), jnp.int16)
+    own = pl.BlockSpec((depth, rows, lanes), lambda i, p: (0, p[0] + i, 0))
+    here = pl.BlockSpec((depth, rows, lanes), lambda i, p: (0, i, 0))
+    return pl.pallas_call(
+        depth_kernel,
+        out_shape=(shape, shape),
+        grid_spec=pltpu.PrefetchScalarGridSpec(
+            num_scalar_prefetch=1,
+            grid=(steps,),
+            in_specs=[pl.BlockSpec((robots, depth, rows, lanes), lambda i, p: (0, 0, p[0] + i, 0)), here, own, own],
+            out_specs=(here, here),
+            scratch_shapes=[
+                pltpu.VMEM((2, depth + 2 * reach, rows, lanes), jnp.float32),
+                pltpu.VMEM((2, depth, rows, lanes), jnp.float32),
+            ],
+        ),
+        compiler_params=pltpu.CompilerParams(vmem_limit_bytes=40 * 2**20),
+        name="depth_pass",
+    )(place, seed_cost, other, occupied, unknown)
+
+
+def envelope(f_ref, h_ref, low_ref, top_ref, mask_ref, extent, tile):
+    blocks = extent // block
+    words = -(-blocks // 32)
+
+    def at(i):
+        return pl.ds(pl.multiple_of(i * tile, tile), tile)
+
+    def own(b, _):
+        g = [f_ref[at(b * block + k), :] for k in range(block)]
+        low = functools.reduce(jnp.minimum, g)
+        low_ref[b] = low
+        top = None
+        for i in range(block):
+            best = functools.reduce(jnp.minimum, [g[j] + float((i - j) ** 2) for j in range(block)])
+            h_ref[at(b * block + i), :] = best
+            top = best if top is None else jnp.maximum(top, best)
+        top_ref[b] = top
+        return 0
+
+    lax.fori_loop(0, blocks, own, 0)
+
+    def bound(b, _):
+        gaps = [jnp.abs(b - j) for j in range(blocks)]
+        top = top_ref[b]
+        for j in range(blocks):
+            reach = (gaps[j] * block + (block - 1)).astype(jnp.float32)
+            top = jnp.minimum(top, low_ref[j] + reach * reach)
+        for word in range(words):
+            bits = jnp.zeros(top.shape, jnp.int32)
+            for j in range(word * 32, min(blocks, word * 32 + 32)):
+                near = ((gaps[j] - 1) * block + 1).astype(jnp.float32)
+                value = 1 << (j % 32)
+                value = value - 2**32 if value >= 2**31 else value
+                bits = bits | jnp.where(low_ref[j] + near * near < top, jnp.int32(value), jnp.int32(0))
+            for axis, size in ((0, tile), (1, 128)):
+                shift = size // 2
+                while shift:
+                    bits = bits | pltpu.roll(bits, shift, axis)
+                    shift //= 2
+            mask_ref[b * words + word] = bits[0, 0]
+        return 0
+
+    lax.fori_loop(0, blocks, bound, 0, unroll=4)
+
+    def outer(b, _):
+        def inner(j, _):
+            wanted = lax.shift_right_logical(mask_ref[b * words + j // 32], j % 32) & 1
+
+            @pl.when((wanted == 1) & (j != b))
+            def _():
+                apart = jnp.full((tile, 128), ((b - j) * block).astype(jnp.float32))
+                square = {}
+                for k in range(1 - block, block):
+                    gap = apart + float(k)
+                    square[k] = gap * gap
+                best = [h_ref[at(b * block + i), :] for i in range(block)]
+                for k in range(block):
+                    g = f_ref[at(j * block + k), :]
+                    best = [jnp.minimum(best[i], g + square[i - k]) for i in range(block)]
+                for i in range(block):
+                    h_ref[at(b * block + i), :] = best[i]
+
+            return 0
+
+        return lax.fori_loop(0, blocks, inner, 0)
+
+    lax.fori_loop(0, blocks, outer, 0)
+
+
+def row_kernel(in_ref, out_ref, f_ref, h_ref, low_ref, top_ref, mask_ref, *, robots):
+    sources, tile, part, _ = in_ref.shape
+    groups = sources // robots
+    extent = sources * part
+    targets, _, wide, _ = out_ref.shape
+    for source in range(sources):
+        start = ((source % groups) * robots + source // groups) * part
+
+        def load(z, _, source=source, start=start):
+            f_ref[pl.ds(start * tile + z, part, stride=tile), :] = decode(in_ref[source, z])
+            return 0
+
+        lax.fori_loop(0, tile, load, 0)
+    envelope(f_ref, h_ref, low_ref, top_ref, mask_ref, extent, tile)
+    for target in range(targets):
+
+        def store(z, _, target=target):
+            out_ref[target, z] = encode(h_ref[pl.ds(target * wide * tile + z, wide, stride=tile), :])
+            return 0
+
+        lax.fori_loop(0, tile, store, 0)
+
+
+def column_kernel(in_ref, *refs):
+    if len(refs) == 7:
+        prior_ref, refs = refs[0], refs[1:]
+    else:
+        prior_ref = None
+    out_ref, f_ref, h_ref, low_ref, top_ref, mask_ref = refs
+    sources, tile, _, part = in_ref.shape
+    for source in range(sources):
+
+        def load(z, _, source=source):
+            f_ref[pl.ds(source * part * tile + z, part, stride=tile), :] = decode(in_ref[source, z]).T
+            return 0
+
+        lax.fori_loop(0, tile, load, 0)
+    envelope(f_ref, h_ref, low_ref, top_ref, mask_ref, sources * part, tile)
+    for source in range(sources):
+        lanes = pl.ds(source * part, part)
+
+        def store(z, _, source=source, lanes=lanes):
+            root = jnp.sqrt(h_ref[pl.ds(source * part * tile + z, part, stride=tile), :]).T
+            if prior_ref is not None:
+                root = voxel_size * (prior_ref[z, :, lanes] - root)
+            out_ref[z, :, lanes] = root
+            return 0
+
+        lax.fori_loop(0, tile, store, 0)
+
+
+def scratch(extent, tile):
+    blocks = extent // block
+    return [
+        pltpu.VMEM((extent * tile, 128), jnp.float32),
+        pltpu.VMEM((extent * tile, 128), jnp.float32),
+        pltpu.VMEM((blocks, tile, 128), jnp.float32),
+        pltpu.VMEM((blocks, tile, 128), jnp.float32),
+        pltpu.SMEM((blocks * -(-blocks // 32),), jnp.int32),
+    ]
+
+
+def whole_call(kernel, shape, extent, tile, name, *operands):
+    vmem = pl.BlockSpec(memory_space=pltpu.VMEM)
+    return pl.pallas_call(
+        kernel,
+        out_shape=shape,
+        in_specs=[vmem] * len(operands),
+        out_specs=vmem,
+        scratch_shapes=scratch(extent, tile),
+        compiler_params=pltpu.CompilerParams(vmem_limit_bytes=40 * 2**20),
+        name=name,
+    )(*operands)
+
+
+def row_pass(received, robots, targets, name):
+    sources, tile, part, lanes = received.shape
+    extent = sources * part
+    shape = jax.ShapeDtypeStruct((targets, tile, extent // targets, lanes), jnp.int16)
+    return whole_call(functools.partial(row_kernel, robots=robots), shape, extent, tile, name, received)
+
+
+def column_pass(received, name, *prior):
+    sources, tile, rows, part = received.shape
+    shape = jax.ShapeDtypeStruct((tile, rows, sources * part), jnp.float32)
+    return whole_call(column_kernel, shape, sources * part, tile, name, received, *prior)
+
+
+def fast_body(seed_cost, occupied, unknown):
+    robots = lax.axis_size("robot")
+    groups = lax.axis_size("xy")
+    strips = lax.axis_size("yz")
+    depth, rows, lanes = occupied.shape
+    half = rows // robots
+    tile = depth // (robots * groups)
+    me = lax.axis_index("robot")
+    for_other = jnp.min(lax.dynamic_slice_in_dim(seed_cost, (1 - me) * half, half, 2), axis=0)
+    other = lax.ppermute(for_other, "robot", [(0, 1), (1, 0)])
+    fields = depth_pass(seed_cost, other, occupied, unknown, half)
+    settled = []
+    for field, label in zip(fields, ("out", "in")):
+        sent = field.reshape(robots * groups, tile, half, lanes)
+        received = lax.all_to_all(sent, ("robot", "xy"), split_axis=0, concat_axis=0, tiled=True)
+        crossed = row_pass(received, robots, strips, "row_pass_" + label)
+        received = lax.all_to_all(crossed, "yz", split_axis=0, concat_axis=0, tiled=True)
+        settled = [column_pass(received, "column_pass_" + label, *settled)]
+    return settled[0]
+
+
+def body(seed_cost, occupied, unknown):
+    robots, groups, strips = (lax.axis_size(name) for name in ("robot", "xy", "yz"))
+    depth, rows, lanes = occupied.shape
+    fits = (
+        robots == 2
+        and seed_cost.shape[0] == 2
+        and lanes == 128
+        and rows % (16 * robots) == 0
+        and depth == 8 * robots * groups
+        and rows * groups == 128 * strips
+        and (depth - 1) ** 2 + largest_cost < penalty
+    )
+    return (fast_body if fits else plain_body)(seed_cost, occupied, unknown)
 
 
 def solution(mesh):

time: 1390 us -> 277 us (0.20)
  other arithmetic: 1130 us -> 2.03 us
  Pallas kernels: 0 us -> 192 us
  waiting for transfers between devices: 157 us -> 23.2 us
  blocking collectives: 51.6 us -> 31.6 us
  local copies, waits for them, and re-layouts: 23.2 us -> 4.38 us
  starting transfers between devices: 5.04 us -> 20.5 us
    reduce_min x4 -> x1, other arithmetic: 1120 us -> 2.03 us  [fast_body(): jnp.min(lax.dynamic_slice_in_dim(seed_cost, (1 - me) * half, half, 2), ax...]
    pallas_call x0 -> x5, Pallas kernels: none -> 192 us  [the longest x4 183 us: whole_call(): pl.pallas_call(kernel, out_shape=shape, in_specs=[vmem] * len(operands),...]
    all_to_all x1 -> x3, waiting for transfers between devices: 91.4 us -> 0.01 us  [the longest x2 0.01 us: fast_body(): lax.all_to_all(crossed, 'yz', split_axis=0, concat_axis=0, tiled=True)]
    pmin x1 -> x0, waiting for transfers between devices: 65.7 us -> none  [body(): merged = lax.pmin(local_lowest, 'robot')]
    ppermute x0 -> x1, waiting for transfers between devices: none -> 23.2 us  [fast_body(): other = lax.ppermute(for_other, 'robot', [(0, 1), (1, 0)])]
    all_to_all x1, blocking collectives: 51.6 us -> 31.6 us  [fast_body(): lax.all_to_all(sent, ('robot', 'xy'), split_axis=0, concat_axis=0, tiled=...]
  transfers between devices with their start and end apart: 2 -> 4, of which waited for: 2 -> 1; matrix products, arithmetic and copies ran while one was open for 0% -> 0% of each run, Pallas kernels for 0% -> 49%
where the time goes in v1:
time: 277 us; the launch traced here: 274 us
  Pallas kernels  192 us (69%)
  blocking collectives  31.6 us (11%)
  waiting for transfers between devices  23.2 us (8%)
  starting transfers between devices  20.5 us (7%)
  local copies, waits for them, and re-layouts  4.38 us (2%)
    pallas_call x4, Pallas kernels, whole_call(): pl.pallas_call(kernel, out_shape=shape, in_specs=[vmem] * len(operands),...  183 us
    all_to_all x1, blocking collectives, fast_body(): lax.all_to_all(sent, ('robot', 'xy'), split_axis=0, concat_axis=0, tiled=...  31.6 us
    ppermute x1, waiting for transfers between devices, fast_body(): other = lax.ppermute(for_other, 'robot', [(0, 1), (1, 0)])  23.2 us
    all_to_all x2, starting transfers between devices, fast_body(): lax.all_to_all(crossed, 'yz', split_axis=0, concat_axis=0, tiled=True)  14 us
    pallas_call x1, Pallas kernels, depth_pass(): pl.pallas_call(depth_kernel, out_shape=(shape, shape), grid_spec=pltpu.Pr...  9.35 us
  transfers between devices with their start and end apart: 4, of which 1 were waited for; matrix products, arithmetic and copies ran while one was open for 0% of the time, Pallas kernels for 49%

profile of v1, /device:TPU:0, one launch (start us, length us, event | category | flops | bytes accessed | tf_op | source)
XLA Modules:
  0.0 273.8 jit_solution(9538710737270334452)
XLA Ops:
  0.0 2.0 dynamic-slice_reduce_fusion
  2.0 3.0 %collective-permute-start = (bf16[64,64,128]{2,1,0:T(8,128)(2,1)S(1)}, bf16[64,64,128]{2,1,0:T(8,128)(2,1)S(1)}, u32[]{:S(2)}, u32[]{:S(2)}) collective-permute-start(bf16[64,64,128]{2,1,0:T(8,128)(2,1)S(1)} %dynamic-slice_reduce_fusion), channel_id=1, source_target_pairs={{0,16},{16,0},{1,17},{17,1},{2,18},{18,2},{3,19},{19,3},{4,20},{20... | collective-permute-start | bytes 3145736 | tf_op jit(solution)/shard_map/ppermute | solution.py:306
  5.0 23.2 %collective-permute-done.other_ref = bf16[64,64,128]{2,1,0:T(8,128)(2,1)S(1)} collective-permute-done((bf16[64,64,128]{2,1,0:T(8,128)(2,1)S(1)}, bf16[64,64,128]{2,1,0:T(8,128)(2,1)S(1)}, u32[]{:S(2)}, u32[]{:S(2)}) %collective-permute-start) | collective-permute-done | bytes 1048608 | tf_op jit(solution)/shard_map/ppermute | solution.py:306
  28.2 0.0 copy-start
  28.2 2.2 copy-done
  30.4 0.0 copy-start.1
  30.4 2.2 copy-done.1
  32.6 9.4 %depth_pass.1 = (s16[64,64,128]{2,1,0:T(8,128)(2,1)S(1)}, s16[64,64,128]{2,1,0:T(8,128)(2,1)}) custom-call(s32[1]{0:T(128)} %bitcast.place_ref, bf16[2,64,128,128]{3,2,1,0:T(8,128)(2,1)S(1)} %copy-done, bf16[64,64,128]{2,1,0:T(8,128)(2,1)S(1)} %collective-permute-done.other_ref, s32[64,128,128]{2,1,0:T(8,128)S(1)} %copy-done.1, s32[64,128,128]{2,1,0:T(8,128)} %unknown_ref.1), custom_call_target="tpu_custom_call" | custom-call | tf_op jit(solution)/shard_map/depth_pass/pallas_call | solution.py:122
  41.9 31.6 %all_to_all.20.in_ref = s16[8,8,64,128]{3,2,1,0:T(8,128)(2,1)S(1)} all-to-all(s16[8,8,64,128]{3,2,1,0:T(8,128)(2,1)S(1)} %bitcast.3), channel_id=1, replica_groups=mesh['robot'=2,'xy'=4,'yz'=4] {'robot','xy'}, dimensions={0} | all-to-all | bytes 2097152 | tf_op jit(solution)/shard_map/all_to_all | solution.py:311
  73.6 3.6 %all-to-all-start = ((s16[8,8,64,128]{3,2,1,0:T(8,128)(2,1)}), s16[8,8,64,128]{3,2,1,0:T(8,128)(2,1)S(1)}, u32[]{:S(2)}, u32[]{:S(2)}) async-start(s16[8,8,64,128]{3,2,1,0:T(8,128)(2,1)} %bitcast.1), calls=%async_computation | async-start | bytes 2097152 | tf_op jit(solution)/shard_map/all_to_all | solution.py:311
  77.1 46.9 %row_pass_out.1 = s16[4,8,128,128]{3,2,1,0:T(8,128)(2,1)} custom-call(s16[8,8,64,128]{3,2,1,0:T(8,128)(2,1)S(1)} %all_to_all.20.in_ref), custom_call_target="tpu_custom_call" | custom-call | tf_op jit(solution)/shard_map/row_pass_out/pallas_call | solution.py:273
  124.1 0.0 all-to-all-done.in_ref
  124.1 9.7 %all-to-all-start.3 = ((s16[4,8,128,128]{3,2,1,0:T(8,128)(2,1)}), s16[4,8,128,128]{3,2,1,0:T(8,128)(2,1)S(1)}, u32[]{:S(2)}, u32[]{:S(2)}) async-start(s16[4,8,128,128]{3,2,1,0:T(8,128)(2,1)} %row_pass_out.1), calls=%async_computation.3 | async-start | bytes 2097152 | tf_op jit(solution)/shard_map/all_to_all | solution.py:313
  133.8 42.9 %row_pass_in.1 = s16[4,8,128,128]{3,2,1,0:T(8,128)(2,1)} custom-call(s16[8,8,64,128]{3,2,1,0:T(8,128)(2,1)S(1)} %all-to-all-done.in_ref), custom_call_target="tpu_custom_call" | custom-call | tf_op jit(solution)/shard_map/row_pass_in/pallas_call | solution.py:273
  176.7 0.0 all-to-all-done.3.in_ref
  176.7 4.2 %all-to-all-start.1 = ((s16[4,8,128,128]{3,2,1,0:T(8,128)(2,1)}), s16[4,8,128,128]{3,2,1,0:T(8,128)(2,1)}, u32[]{:S(2)}, u32[]{:S(2)}) async-start(s16[4,8,128,128]{3,2,1,0:T(8,128)(2,1)} %row_pass_in.1), calls=%async_computation.1 | async-start | bytes 2097152 | tf_op jit(solution)/shard_map/all_to_all | solution.py:313
  180.9 44.9 %column_pass_out.1.refs_0_ = f32[8,128,512]{2,1,0:T(8,128)S(1)} custom-call(s16[4,8,128,128]{3,2,1,0:T(8,128)(2,1)S(1)} %all-to-all-done.3.in_ref), custom_call_target="tpu_custom_call" | custom-call | tf_op jit(solution)/shard_map/column_pass_out/pallas_call | solution.py:273
  225.8 0.0 all-to-all-done.1.in_ref
  225.8 48.0 %column_pass_in.1 = f32[8,128,512]{2,1,0:T(8,128)} custom-call(s16[4,8,128,128]{3,2,1,0:T(8,128)(2,1)} %all-to-all-done.1.in_ref, f32[8,128,512]{2,1,0:T(8,128)S(1)} %column_pass_out.1.refs_0_), custom_call_target="tpu_custom_call" | custom-call | tf_op jit(solution)/shard_map/column_pass_in/pallas_call | solution.py:273
Async XLA Ops:
  2.0 26.2 %collective-permute-start = (bf16[64,64,128]{2,1,0:T(8,128)(2,1)S(1)}, bf16[64,64,128]{2,1,0:T(8,128)(2,1)S(1)}, u32[]{:S(2)}, u32[]{:S(2)}) collective-permute-start(bf16[64,64,128]{2,1,0:T(8,128)(2,1)S(1)} %dynamic-slice_reduce_fusion), channel_id=1, source_target_pairs={{0,16},{16,0},{1,17},{17,1},{2,18},{18,2},{3,19},{19,3},{4,20},{20... | collective-permute-start | bytes 3145736 | tf_op jit(solution)/shard_map/ppermute | solution.py:306
  28.2 2.2 copy-start
  30.4 2.2 copy-start.1
  73.6 50.5 %all-to-all-start = ((s16[8,8,64,128]{3,2,1,0:T(8,128)(2,1)}), s16[8,8,64,128]{3,2,1,0:T(8,128)(2,1)S(1)}, u32[]{:S(2)}, u32[]{:S(2)}) async-start(s16[8,8,64,128]{3,2,1,0:T(8,128)(2,1)} %bitcast.1), calls=%async_computation | async-start | bytes 2097152 | tf_op jit(solution)/shard_map/all_to_all | solution.py:311
  124.1 52.6 %all-to-all-start.3 = ((s16[4,8,128,128]{3,2,1,0:T(8,128)(2,1)}), s16[4,8,128,128]{3,2,1,0:T(8,128)(2,1)S(1)}, u32[]{:S(2)}, u32[]{:S(2)}) async-start(s16[4,8,128,128]{3,2,1,0:T(8,128)(2,1)} %row_pass_out.1), calls=%async_computation.3 | async-start | bytes 2097152 | tf_op jit(solution)/shard_map/all_to_all | solution.py:313
  176.7 49.1 %all-to-all-start.1 = ((s16[4,8,128,128]{3,2,1,0:T(8,128)(2,1)}), s16[4,8,128,128]{3,2,1,0:T(8,128)(2,1)}, u32[]{:S(2)}, u32[]{:S(2)}) async-start(s16[4,8,128,128]{3,2,1,0:T(8,128)(2,1)} %row_pass_in.1), calls=%async_computation.1 | async-start | bytes 2097152 | tf_op jit(solution)/shard_map/all_to_all | solution.py:313

commit v2 on v1

--- a/solution.py
+++ b/solution.py
@@ -15,6 +15,7 @@
 codes = 65535.0
 span = math.log(1.0 + sharpness * (penalty + 1024.0))
 block = 16
+margin = 8
 far_away = 4194304.0
 
 
@@ -132,139 +133,157 @@
                 pltpu.VMEM((2, depth, rows, lanes), jnp.float32),
             ],
         ),
-        compiler_params=pltpu.CompilerParams(vmem_limit_bytes=40 * 2**20),
+        compiler_params=pltpu.CompilerParams(vmem_limit_bytes=56 * 2**20),
         name="depth_pass",
     )(place, seed_cost, other, occupied, unknown)
 
 
-def envelope(f_ref, h_ref, low_ref, top_ref, mask_ref, extent, tile):
+def envelope(f_ref, h_ref, low_ref, top_ref, bits_ref, reach_ref, near_ref, list_ref, extent, tile):
     blocks = extent // block
     words = -(-blocks // 32)
 
-    def at(i):
+    def source(j):
+        return pl.ds(pl.multiple_of((margin + j) * tile, tile), tile)
+
+    def target(i):
         return pl.ds(pl.multiple_of(i * tile, tile), tile)
 
+    for pad in range(margin):
+        for place in (pad, margin + extent + pad):
+            f_ref[place * tile : (place + 1) * tile, :] = jnp.full((tile, 128), far_away, jnp.float32)
+    for gap in range(blocks):
+        reach = float((gap * block + block - 1) ** 2)
+        near = float((gap - 1) * block + 1) ** 2 if gap > 1 else float((margin + 1) ** 2) if gap else 2 * far_away
+        for index in {blocks - gap, blocks + gap}:
+            reach_ref[index] = jnp.full((tile, 128), reach, jnp.float32)
+            near_ref[index] = jnp.full((tile, 128), near, jnp.float32)
+
     def own(b, _):
-        g = [f_ref[at(b * block + k), :] for k in range(block)]
-        low = functools.reduce(jnp.minimum, g)
-        low_ref[b] = low
+        g = [f_ref[source(b * block + k - margin), :] for k in range(block + 2 * margin)]
+        low_ref[b] = functools.reduce(jnp.minimum, g[margin : margin + block])
         top = None
         for i in range(block):
-            best = functools.reduce(jnp.minimum, [g[j] + float((i - j) ** 2) for j in range(block)])
-            h_ref[at(b * block + i), :] = best
+            best = g[margin + i]
+            for j in range(block + 2 * margin):
+                apart = abs(j - margin - i)
+                if apart and (apart <= margin or 0 <= j - margin < block):
+                    best = jnp.minimum(best, g[j] + float(apart**2))
+            h_ref[target(b * block + i), :] = best
             top = best if top is None else jnp.maximum(top, best)
         top_ref[b] = top
         return 0
 
     lax.fori_loop(0, blocks, own, 0)
 
-    def bound(b, _):
-        gaps = [jnp.abs(b - j) for j in range(blocks)]
-        top = top_ref[b]
-        for j in range(blocks):
-            reach = (gaps[j] * block + (block - 1)).astype(jnp.float32)
-            top = jnp.minimum(top, low_ref[j] + reach * reach)
+    def bound(group, count):
+        for r in range(8):
+            b = group * 8 + r
+            top = top_ref[b]
+            for j in range(blocks):
+                top = jnp.minimum(top, low_ref[j] + reach_ref[blocks + b - j])
+            for word in range(words):
+                bits = jnp.zeros(top.shape, jnp.int32)
+                for j in range(word * 32, min(blocks, word * 32 + 32)):
+                    value = 1 << (j % 32)
+                    value = value - 2**32 if value >= 2**31 else value
+                    bits = bits | jnp.where(low_ref[j] + near_ref[blocks + b - j] < top, jnp.int32(value), jnp.int32(0))
+                bits_ref[word, pl.ds(r * tile, tile), :] = bits
         for word in range(words):
-            bits = jnp.zeros(top.shape, jnp.int32)
-            for j in range(word * 32, min(blocks, word * 32 + 32)):
-                near = ((gaps[j] - 1) * block + 1).astype(jnp.float32)
-                value = 1 << (j % 32)
-                value = value - 2**32 if value >= 2**31 else value
-                bits = bits | jnp.where(low_ref[j] + near * near < top, jnp.int32(value), jnp.int32(0))
-            for axis, size in ((0, tile), (1, 128)):
-                shift = size // 2
-                while shift:
-                    bits = bits | pltpu.roll(bits, shift, axis)
-                    shift //= 2
-            mask_ref[b * words + word] = bits[0, 0]
-        return 0
-
-    lax.fori_loop(0, blocks, bound, 0, unroll=4)
-
-    def outer(b, _):
-        def inner(j, _):
-            wanted = lax.shift_right_logical(mask_ref[b * words + j // 32], j % 32) & 1
-
-            @pl.when((wanted == 1) & (j != b))
-            def _():
-                apart = jnp.full((tile, 128), ((b - j) * block).astype(jnp.float32))
-                square = {}
-                for k in range(1 - block, block):
-                    gap = apart + float(k)
-                    square[k] = gap * gap
-                best = [h_ref[at(b * block + i), :] for i in range(block)]
-                for k in range(block):
-                    g = f_ref[at(j * block + k), :]
-                    best = [jnp.minimum(best[i], g + square[i - k]) for i in range(block)]
-                for i in range(block):
-                    h_ref[at(b * block + i), :] = best[i]
-
-            return 0
-
-        return lax.fori_loop(0, blocks, inner, 0)
-
-    lax.fori_loop(0, blocks, outer, 0)
-
-
-def row_kernel(in_ref, out_ref, f_ref, h_ref, low_ref, top_ref, mask_ref, *, robots):
+            joined = functools.reduce(jnp.bitwise_or, [bits_ref[word, pl.ds(k, 8, stride=tile), :] for k in range(tile)])
+            shift = 64
+            while shift:
+                joined = joined | pltpu.roll(joined, shift, 1)
+                shift //= 2
+            for r in range(8):
+                mask = joined[r, 0]
+                for j in range(word * 32, min(blocks, word * 32 + 32)):
+                    list_ref[count] = (group * 8 + r) * 1024 + j
+                    count = count + (lax.shift_right_logical(mask, j % 32) & 1)
+        return count
+
+    count = lax.fori_loop(0, blocks // 8, bound, jnp.int32(0))
+
+    def visit(k, _):
+        code = list_ref[k]
+        b = lax.shift_right_logical(code, 10)
+        j = code & 1023
+        apart = jnp.full((tile, 128), ((b - j) * block).astype(jnp.float32))
+        square = {}
+        for step in range(1 - block, block):
+            gap = apart + float(step)
+            square[step] = gap * gap
+        best = [h_ref[target(b * block + i), :] for i in range(block)]
+        for step in range(block):
+            g = f_ref[source(j * block + step), :]
+            best = [jnp.minimum(best[i], g + square[i - step]) for i in range(block)]
+        for i in range(block):
+            h_ref[target(b * block + i), :] = best[i]
+        return 0
+
+    lax.fori_loop(0, count, visit, 0)
+
+
+def row_kernel(in_ref, out_ref, f_ref, h_ref, *rest, robots):
     sources, tile, part, _ = in_ref.shape
     groups = sources // robots
     extent = sources * part
     targets, _, wide, _ = out_ref.shape
-    for source in range(sources):
-        start = ((source % groups) * robots + source // groups) * part
-
-        def load(z, _, source=source, start=start):
-            f_ref[pl.ds(start * tile + z, part, stride=tile), :] = decode(in_ref[source, z])
-            return 0
-
-        lax.fori_loop(0, tile, load, 0)
-    envelope(f_ref, h_ref, low_ref, top_ref, mask_ref, extent, tile)
-    for target in range(targets):
-
-        def store(z, _, target=target):
+
+    def load(source, _):
+        start = (margin + (lax.rem(source, groups) * robots + source // groups) * part) * tile
+        for z in range(tile):
+            f_ref[pl.ds(start + z, part, stride=tile), :] = decode(in_ref[source, z])
+        return 0
+
+    lax.fori_loop(0, sources, load, 0)
+    envelope(f_ref, h_ref, *rest, extent, tile)
+
+    def store(target, _):
+        for z in range(tile):
             out_ref[target, z] = encode(h_ref[pl.ds(target * wide * tile + z, wide, stride=tile), :])
-            return 0
-
-        lax.fori_loop(0, tile, store, 0)
-
-
-def column_kernel(in_ref, *refs):
-    if len(refs) == 7:
-        prior_ref, refs = refs[0], refs[1:]
-    else:
-        prior_ref = None
-    out_ref, f_ref, h_ref, low_ref, top_ref, mask_ref = refs
+        return 0
+
+    lax.fori_loop(0, targets, store, 0)
+
+
+def column_kernel(in_ref, *refs, has_prior):
+    prior_ref, refs = (refs[0], refs[1:]) if has_prior else (None, refs)
+    out_ref, f_ref, h_ref, *rest = refs
     sources, tile, _, part = in_ref.shape
-    for source in range(sources):
-
-        def load(z, _, source=source):
-            f_ref[pl.ds(source * part * tile + z, part, stride=tile), :] = decode(in_ref[source, z]).T
-            return 0
-
-        lax.fori_loop(0, tile, load, 0)
-    envelope(f_ref, h_ref, low_ref, top_ref, mask_ref, sources * part, tile)
-    for source in range(sources):
-        lanes = pl.ds(source * part, part)
-
-        def store(z, _, source=source, lanes=lanes):
+
+    def load(z, _):
+        for source in range(sources):
+            start = (margin + source * part) * tile
+            f_ref[pl.ds(start + z, part, stride=tile), :] = decode(in_ref[source, z]).T
+        return 0
+
+    lax.fori_loop(0, tile, load, 0)
+    envelope(f_ref, h_ref, *rest, sources * part, tile)
+
+    def store(z, _):
+        for source in range(sources):
+            lanes = pl.ds(source * part, part)
             root = jnp.sqrt(h_ref[pl.ds(source * part * tile + z, part, stride=tile), :]).T
-            if prior_ref is not None:
+            if has_prior:
                 root = voxel_size * (prior_ref[z, :, lanes] - root)
             out_ref[z, :, lanes] = root
-            return 0
-
-        lax.fori_loop(0, tile, store, 0)
+        return 0
+
+    lax.fori_loop(0, tile, store, 0)
 
 
 def scratch(extent, tile):
     blocks = extent // block
+    words = -(-blocks // 32)
     return [
-        pltpu.VMEM((extent * tile, 128), jnp.float32),
+        pltpu.VMEM(((extent + 2 * margin) * tile, 128), jnp.float32),
         pltpu.VMEM((extent * tile, 128), jnp.float32),
         pltpu.VMEM((blocks, tile, 128), jnp.float32),
         pltpu.VMEM((blocks, tile, 128), jnp.float32),
-        pltpu.SMEM((blocks * -(-blocks // 32),), jnp.int32),
+        pltpu.VMEM((words, 8 * tile, 128), jnp.int32),
+        pltpu.VMEM((2 * blocks, tile, 128), jnp.float32),
+        pltpu.VMEM((2 * blocks, tile, 128), jnp.float32),
+        pltpu.SMEM((blocks * blocks + 1,), jnp.int32),
     ]
 
 
@@ -276,7 +295,7 @@
         in_specs=[vmem] * len(operands),
         out_specs=vmem,
         scratch_shapes=scratch(extent, tile),
-        compiler_params=pltpu.CompilerParams(vmem_limit_bytes=40 * 2**20),
+        compiler_params=pltpu.CompilerParams(vmem_limit_bytes=56 * 2**20),
         name=name,
     )(*operands)
 
@@ -291,7 +310,7 @@
 def column_pass(received, name, *prior):
     sources, tile, rows, part = received.shape
     shape = jax.ShapeDtypeStruct((tile, rows, sources * part), jnp.float32)
-    return whole_call(column_kernel, shape, sources * part, tile, name, received, *prior)
+    return whole_call(functools.partial(column_kernel, has_prior=bool(prior)), shape, sources * part, tile, name, received, *prior)
 
 
 def fast_body(seed_cost, occupied, unknown):
@@ -325,6 +344,7 @@
         and rows % (16 * robots) == 0
         and depth == 8 * robots * groups
         and rows * groups == 128 * strips
+        and rows * groups % (8 * block) == 0
         and (depth - 1) ** 2 + largest_cost < penalty
     )
     return (fast_body if fits else plain_body)(seed_cost, occupied, unknown)

time: 277 us -> 154 us (0.56)
  Pallas kernels: 192 us -> 73.8 us
  starting transfers between devices: 20.5 us -> 13.6 us
  waiting for transfers between devices: 23.2 us -> 28.7 us
    pallas_call x4, Pallas kernels: 183 us -> 64.3 us  [whole_call(): pl.pallas_call(kernel, out_shape=shape, in_specs=[vmem] * len(operands),...]
    all_to_all x2, starting transfers between devices: 14 us -> 7.03 us  [fast_body(): lax.all_to_all(crossed, 'yz', split_axis=0, concat_axis=0, tiled=True)]
    all_to_all x1, waiting for transfers between devices: 0.01 us -> 4.93 us  [fast_body(): lax.all_to_all(sent, ('robot', 'xy'), split_axis=0, concat_axis=0, tiled=...]
  transfers between devices with their start and end apart: 4 -> 4, of which waited for: 1 -> 3; matrix products, arithmetic and copies ran while one was open for 0% -> 0% of each run, Pallas kernels for 49% -> 33%
where the time goes in v2:
time: 154 us; the launch traced here: 152 us
  Pallas kernels  73.8 us (48%)
  blocking collectives  31.9 us (21%)
  waiting for transfers between devices  28.7 us (19%)
  starting transfers between devices  13.6 us (9%)
  other arithmetic  2.03 us (1%)
  local copies, waits for them, and re-layouts  1.96 us (1%)
    pallas_call x4, Pallas kernels, whole_call(): pl.pallas_call(kernel, out_shape=shape, in_specs=[vmem] * len(operands),...  64.3 us
    all_to_all x1, blocking collectives, fast_body(): lax.all_to_all(sent, ('robot', 'xy'), split_axis=0, concat_axis=0, tiled=...  31.9 us
    ppermute x1, waiting for transfers between devices, fast_body(): other = lax.ppermute(for_other, 'robot', [(0, 1), (1, 0)])  23.2 us
    pallas_call x1, Pallas kernels, depth_pass(): pl.pallas_call(depth_kernel, out_shape=(shape, shape), grid_spec=pltpu.Pr...  9.46 us
    all_to_all x2, starting transfers between devices, fast_body(): lax.all_to_all(crossed, 'yz', split_axis=0, concat_axis=0, tiled=True)  7.03 us
    all_to_all x1, waiting for transfers between devices, fast_body(): lax.all_to_all(sent, ('robot', 'xy'), split_axis=0, concat_axis=0, tiled=...  4.93 us
    all_to_all x1, starting transfers between devices, fast_body(): lax.all_to_all(sent, ('robot', 'xy'), split_axis=0, concat_axis=0, tiled=...  3.56 us
  transfers between devices with their start and end apart: 4, of which 3 were waited for; matrix products, arithmetic and copies ran while one was open for 0% of the time, Pallas kernels for 33%

profile of v2, /device:TPU:0, one launch (start us, length us, event | category | flops | bytes accessed | tf_op | source)
XLA Modules:
  0.0 152.1 jit_solution(10550208719852484061)
XLA Ops:
  0.0 2.0 %dynamic-slice_reduce_fusion = bf16[64,64,128]{2,1,0:T(8,128)(2,1)S(1)} fusion(bf16[2,64,128,128]{3,2,1,0:T(8,128)(2,1)} %cost_ref.1, s32[]{:T(128)S(6)} %select_n.3), kind=kLoop, calls=%fused_computation | loop fusion | flops 524288 | bytes 3145732 | tf_op jit(solution)/shard_map/reduce_min | solution.py:324
  2.0 3.0 %collective-permute-start = (bf16[64,64,128]{2,1,0:T(8,128)(2,1)S(1)}, bf16[64,64,128]{2,1,0:T(8,128)(2,1)S(1)}, u32[]{:S(2)}, u32[]{:S(2)}) collective-permute-start(bf16[64,64,128]{2,1,0:T(8,128)(2,1)S(1)} %dynamic-slice_reduce_fusion), channel_id=1, source_target_pairs={{0,16},{16,0},{1,17},{17,1},{2,18},{18,2},{3,19},{19,3},{4,20},{20... | collective-permute-start | bytes 3145736 | tf_op jit(solution)/shard_map/ppermute | solution.py:325
  5.0 23.2 %collective-permute-done.other_ref = bf16[64,64,128]{2,1,0:T(8,128)(2,1)S(1)} collective-permute-done((bf16[64,64,128]{2,1,0:T(8,128)(2,1)S(1)}, bf16[64,64,128]{2,1,0:T(8,128)(2,1)S(1)}, u32[]{:S(2)}, u32[]{:S(2)}) %collective-permute-start) | collective-permute-done | bytes 1048608 | tf_op jit(solution)/shard_map/ppermute | solution.py:325
  28.2 0.0 copy-start.3
  28.2 1.0 copy-done.3
  29.2 9.5 %depth_pass.1 = (s16[64,64,128]{2,1,0:T(8,128)(2,1)}, s16[64,64,128]{2,1,0:T(8,128)(2,1)}) custom-call(s32[1]{0:T(128)} %bitcast.place_ref, bf16[2,64,128,128]{3,2,1,0:T(8,128)(2,1)} %cost_ref.1, bf16[64,64,128]{2,1,0:T(8,128)(2,1)} %copy-done.3, s32[64,128,128]{2,1,0:T(8,128)} %occupied_ref.1, s32[64,128,128]{2,1,0:T(8,128)} %unknown_ref.1), custom_call_target="tpu_custom_call" | custom-call | tf_op jit(solution)/shard_map/depth_pass/pallas_call | solution.py:123
  38.6 31.9 %all_to_all.20.in_ref = s16[8,8,64,128]{3,2,1,0:T(8,128)(2,1)} all-to-all(s16[8,8,64,128]{3,2,1,0:T(8,128)(2,1)} %bitcast.4), channel_id=1, replica_groups=mesh['robot'=2,'xy'=4,'yz'=4] {'robot','xy'}, dimensions={0} | all-to-all | bytes 2097152 | tf_op jit(solution)/shard_map/all_to_all | solution.py:330
  70.6 3.6 %all-to-all-start = ((s16[8,8,64,128]{3,2,1,0:T(8,128)(2,1)}), s16[8,8,64,128]{3,2,1,0:T(8,128)(2,1)S(1)}, u32[]{:S(2)}, u32[]{:S(2)}) async-start(s16[8,8,64,128]{3,2,1,0:T(8,128)(2,1)} %bitcast.3), calls=%async_computation | async-start | bytes 2097152 | tf_op jit(solution)/shard_map/all_to_all | solution.py:330
  74.1 20.1 %row_pass_out.1 = s16[4,8,128,128]{3,2,1,0:T(8,128)(2,1)} custom-call(s16[8,8,64,128]{3,2,1,0:T(8,128)(2,1)} %all_to_all.20.in_ref), custom_call_target="tpu_custom_call" | custom-call | tf_op jit(solution)/shard_map/row_pass_out/pallas_call | solution.py:292
  94.3 4.9 %all-to-all-done.in_ref = s16[8,8,64,128]{3,2,1,0:T(8,128)(2,1)S(1)} async-done(((s16[8,8,64,128]{3,2,1,0:T(8,128)(2,1)}), s16[8,8,64,128]{3,2,1,0:T(8,128)(2,1)S(1)}, u32[]{:S(2)}, u32[]{:S(2)}) %all-to-all-start) | async-done | bytes 1048608 | tf_op jit(solution)/shard_map/all_to_all | solution.py:330
  99.2 0.0 copy-start.2
  99.2 3.5 %all-to-all-start.3 = ((s16[4,8,128,128]{3,2,1,0:T(8,128)(2,1)}), s16[4,8,128,128]{3,2,1,0:T(8,128)(2,1)S(1)}, u32[]{:S(2)}, u32[]{:S(2)}) async-start(s16[4,8,128,128]{3,2,1,0:T(8,128)(2,1)} %row_pass_out.1), calls=%async_computation.3 | async-start | bytes 2097152 | tf_op jit(solution)/shard_map/all_to_all | solution.py:332
  102.7 0.0 copy-done.2
  102.7 13.8 %row_pass_in.1 = s16[4,8,128,128]{3,2,1,0:T(8,128)(2,1)} custom-call(s16[8,8,64,128]{3,2,1,0:T(8,128)(2,1)} %copy-done.2), custom_call_target="tpu_custom_call" | custom-call | tf_op jit(solution)/shard_map/row_pass_in/pallas_call | solution.py:292
  116.5 0.6 all-to-all-done.3.in_ref
  117.1 0.0 copy-start
  117.2 3.5 %all-to-all-start.1 = ((s16[4,8,128,128]{3,2,1,0:T(8,128)(2,1)}), s16[4,8,128,128]{3,2,1,0:T(8,128)(2,1)S(1)}, u32[]{:S(2)}, u32[]{:S(2)}) async-start(s16[4,8,128,128]{3,2,1,0:T(8,128)(2,1)} %row_pass_in.1), calls=%async_computation.1 | async-start | bytes 2097152 | tf_op jit(solution)/shard_map/all_to_all | solution.py:332
  120.7 0.0 copy-done
  120.7 16.2 %column_pass_out.1.refs_0_ = f32[8,128,512]{2,1,0:T(8,128)} custom-call(s16[4,8,128,128]{3,2,1,0:T(8,128)(2,1)} %copy-done), custom_call_target="tpu_custom_call" | custom-call | tf_op jit(solution)/shard_map/column_pass_out/pallas_call | solution.py:292
  136.9 0.0 all-to-all-done.1.in_ref
  136.9 0.0 copy-start.1
  136.9 1.0 copy-done.1
  137.8 14.2 %column_pass_in.1 = f32[8,128,512]{2,1,0:T(8,128)} custom-call(s16[4,8,128,128]{3,2,1,0:T(8,128)(2,1)} %copy-done.1, f32[8,128,512]{2,1,0:T(8,128)} %column_pass_out.1.refs_0_), custom_call_target="tpu_custom_call" | custom-call | tf_op jit(solution)/shard_map/column_pass_in/pallas_call | solution.py:292
Async XLA Ops:
  2.0 26.2 %collective-permute-start = (bf16[64,64,128]{2,1,0:T(8,128)(2,1)S(1)}, bf16[64,64,128]{2,1,0:T(8,128)(2,1)S(1)}, u32[]{:S(2)}, u32[]{:S(2)}) collective-permute-start(bf16[64,64,128]{2,1,0:T(8,128)(2,1)S(1)} %dynamic-slice_reduce_fusion), channel_id=1, source_target_pairs={{0,16},{16,0},{1,17},{17,1},{2,18},{18,2},{3,19},{19,3},{4,20},{20... | collective-permute-start | bytes 3145736 | tf_op jit(solution)/shard_map/ppermute | solution.py:325
  28.2 1.0 copy-start.3
  70.6 28.6 %all-to-all-start = ((s16[8,8,64,128]{3,2,1,0:T(8,128)(2,1)}), s16[8,8,64,128]{3,2,1,0:T(8,128)(2,1)S(1)}, u32[]{:S(2)}, u32[]{:S(2)}) async-start(s16[8,8,64,128]{3,2,1,0:T(8,128)(2,1)} %bitcast.3), calls=%async_computation | async-start | bytes 2097152 | tf_op jit(solution)/shard_map/all_to_all | solution.py:330
  99.2 3.5 %copy-start.2 = (s16[8,8,64,128]{3,2,1,0:T(8,128)(2,1)}, s16[8,8,64,128]{3,2,1,0:T(8,128)(2,1)S(1)}, u32[]{:S(2)}) copy-start(s16[8,8,64,128]{3,2,1,0:T(8,128)(2,1)S(1)} %all-to-all-done.in_ref) | copy-start | bytes 3145732
  99.2 18.0 %all-to-all-start.3 = ((s16[4,8,128,128]{3,2,1,0:T(8,128)(2,1)}), s16[4,8,128,128]{3,2,1,0:T(8,128)(2,1)S(1)}, u32[]{:S(2)}, u32[]{:S(2)}) async-start(s16[4,8,128,128]{3,2,1,0:T(8,128)(2,1)} %row_pass_out.1), calls=%async_computation.3 | async-start | bytes 2097152 | tf_op jit(solution)/shard_map/all_to_all | solution.py:332
  117.1 3.5 %copy-start = (s16[4,8,128,128]{3,2,1,0:T(8,128)(2,1)}, s16[4,8,128,128]{3,2,1,0:T(8,128)(2,1)S(1)}, u32[]{:S(2)}) copy-start(s16[4,8,128,128]{3,2,1,0:T(8,128)(2,1)S(1)} %all-to-all-done.3.in_ref) | copy-start | bytes 3145732
  117.2 19.7 %all-to-all-start.1 = ((s16[4,8,128,128]{3,2,1,0:T(8,128)(2,1)}), s16[4,8,128,128]{3,2,1,0:T(8,128)(2,1)S(1)}, u32[]{:S(2)}, u32[]{:S(2)}) async-start(s16[4,8,128,128]{3,2,1,0:T(8,128)(2,1)} %row_pass_in.1), calls=%async_computation.1 | async-start | bytes 2097152 | tf_op jit(solution)/shard_map/all_to_all | solution.py:332
  136.9 1.0 copy-start.1

commit v3 on v2

--- a/solution.py
+++ b/solution.py
@@ -63,79 +63,186 @@
     return (jnp.exp(scaled * (span / codes)) - 1.0) * (1.0 / sharpness)
 
 
-def depth_kernel(place_ref, cost_ref, other_ref, occupied_ref, unknown_ref, out_ref, in_ref, g_ref, h_ref):
-    depth = other_ref.shape[0]
-    rows, lanes = other_ref.shape[1:]
+def depth_kernel(
+    cost_ref, occupied_ref, unknown_ref, out_ref, in_ref,
+    cost_other, cost_own, occupied_own, unknown_own, gone, come, code, g_ref, h_ref,
+    other_sem, own_sem, gone_sem, come_sem, send_sem, recv_sem, keep_sem,
+):
+    robots, groups = lax.axis_size("robot"), lax.axis_size("xy")
+    robot, group = lax.axis_index("robot"), lax.axis_index("xy")
+    members = robots * groups
+    me = robot * groups + group
+    chunks, depth, rows, lanes = gone.shape
+    half = chunks * rows
+    tile = depth // members
     reach = math.isqrt(int(largest_cost)) + 1
+
+    def place(member):
+        return {"robot": member // groups, "xy": lax.rem(member, groups)}
+
+    def span_of(owner, c):
+        return pl.ds(pl.multiple_of(owner * half + c * rows, rows), rows)
+
+    def fetch_other(c):
+        return pltpu.make_async_copy(cost_ref.at[:, :, span_of(1 - robot, c), :], cost_other.at[c], other_sem.at[c])
+
+    def fetch_own(c):
+        return (
+            pltpu.make_async_copy(cost_ref.at[:, :, span_of(robot, c), :], cost_own.at[c], own_sem.at[0, c]),
+            pltpu.make_async_copy(occupied_ref.at[:, span_of(robot, c), :], occupied_own.at[c], own_sem.at[1, c]),
+            pltpu.make_async_copy(unknown_ref.at[:, span_of(robot, c), :], unknown_own.at[c], own_sem.at[2, c]),
+        )
+
+    def hand_over(c):
+        return pltpu.make_async_remote_copy(
+            src_ref=gone.at[c], dst_ref=come.at[c], send_sem=gone_sem.at[c], recv_sem=come_sem.at[c],
+            device_id={"robot": 1 - robot}, device_id_type=pl.DeviceIdType.MESH,
+        )
+
+    def send(c, step):
+        member = lax.rem(me + step, members)
+        return pltpu.make_async_remote_copy(
+            src_ref=code.at[0, c, pl.ds(member * tile, tile)], dst_ref=out_ref.at[me, :, span_of(0, c), :],
+            send_sem=send_sem.at[c, step - 1], recv_sem=recv_sem.at[c, step - 1],
+            device_id=place(member), device_id_type=pl.DeviceIdType.MESH,
+        )
+
+    def keep(c):
+        return (
+            pltpu.make_async_copy(code.at[0, c, pl.ds(me * tile, tile)], out_ref.at[me, :, span_of(0, c), :], keep_sem.at[0, c]),
+            pltpu.make_async_copy(code.at[1, c], in_ref.at[:, span_of(0, c), :], keep_sem.at[1, c]),
+        )
+
+    def over_chunks(do):
+        def step(c, _):
+            do(c)
+            return 0
+
+        lax.fori_loop(0, chunks, step, 0)
+
+    def begin(c):
+        fetch_other(c).start()
+
+    over_chunks(begin)
+
+    def begin_own(c):
+        for copy in fetch_own(c):
+            copy.start()
+
+    over_chunks(begin_own)
+
+    barrier = pltpu.get_barrier_semaphore()
+    for step in range(1, members):
+        pl.semaphore_signal(barrier, inc=1, device_id=place(lax.rem(me + step, members)), device_id_type=pl.DeviceIdType.MESH)
+    pl.semaphore_wait(barrier, members - 1)
+
+    def merge(c):
+        fetch_other(c).wait()
+        gone[c] = jnp.minimum(cost_other[c, 0], cost_other[c, 1])
+        hand_over(c).start()
+
+    over_chunks(merge)
+
     wall = jnp.full((rows, lanes), far_away, jnp.float32)
+    nothing = jnp.zeros((rows, lanes), jnp.float32)
     for field in range(2):
         for pad in range(reach):
             g_ref[field, pad] = wall
             g_ref[field, depth + reach + pad] = wall
 
-    def seeds(z, carry):
-        merged = jnp.minimum(jnp.minimum(cost_ref[0, z], cost_ref[1, z]), other_ref[z]).astype(jnp.float32)
-        occupied = occupied_ref[z] == 1
-        blocked = occupied | (unknown_ref[z] == 1)
-        fields = (jnp.where(occupied, merged, merged + penalty), jnp.where(blocked, merged + penalty, merged))
-        after = []
-        for field, (cost, away) in zip(range(2), carry):
-            value = fields[field]
-            g_ref[field, z + reach] = value
-            seed = value < penalty
-            cost = jnp.where(seed, value, cost)
-            away = jnp.where(seed, 0.0, away + 1.0)
-            h_ref[field, z] = cost + away * away
-            after.append((cost, away))
-        return tuple(after)
-
-    nothing = jnp.zeros((rows, lanes), jnp.float32)
-    lax.fori_loop(0, depth, seeds, ((wall, nothing), (wall, nothing)), unroll=4)
-
-    def settle(step, carry):
-        z = depth - 1 - step
-        after = []
-        for field, (cost, away) in zip(range(2), carry):
-            value = g_ref[field, z + reach]
-            seed = value < penalty
-            cost = jnp.where(seed, value, cost)
-            away = jnp.where(seed, 0.0, away + 1.0)
-            best = jnp.minimum(jnp.minimum(h_ref[field, z], cost + away * away), value)
-            for apart in range(1, reach + 1):
-                pair = jnp.minimum(g_ref[field, z + reach - apart], g_ref[field, z + reach + apart])
-                best = jnp.minimum(best, pair + float(apart * apart))
-            (out_ref, in_ref)[field][z] = encode(best)
-            after.append((cost, away))
-        return tuple(after)
-
-    lax.fori_loop(0, depth, settle, ((wall, nothing), (wall, nothing)), unroll=4)
-
-
-def depth_pass(seed_cost, other, occupied, unknown, half):
+    def pass_chunk(c):
+        for copy in fetch_own(c):
+            copy.wait()
+        hand_over(c).wait_recv()
+
+        def seeds(z, carry):
+            merged = jnp.minimum(jnp.minimum(cost_own[c, 0, z], cost_own[c, 1, z]), come[c, z]).astype(jnp.float32)
+            occupied = occupied_own[c, z] == 1
+            blocked = occupied | (unknown_own[c, z] == 1)
+            fields = (jnp.where(occupied, merged, merged + penalty), jnp.where(blocked, merged + penalty, merged))
+            after = []
+            for field, (cost, away) in zip(range(2), carry):
+                value = fields[field]
+                g_ref[field, z + reach] = value
+                seed = value < penalty
+                cost = jnp.where(seed, value, cost)
+                away = jnp.where(seed, 0.0, away + 1.0)
+                h_ref[field, z] = cost + away * away
+                after.append((cost, away))
+            return tuple(after)
+
+        lax.fori_loop(0, depth, seeds, ((wall, nothing), (wall, nothing)), unroll=4)
+
+        def settle(step, carry):
+            z = depth - 1 - step
+            after = []
+            for field, (cost, away) in zip(range(2), carry):
+                value = g_ref[field, z + reach]
+                seed = value < penalty
+                cost = jnp.where(seed, value, cost)
+                away = jnp.where(seed, 0.0, away + 1.0)
+                best = jnp.minimum(jnp.minimum(h_ref[field, z], cost + away * away), value)
+                for apart in range(1, reach + 1):
+                    pair = jnp.minimum(g_ref[field, z + reach - apart], g_ref[field, z + reach + apart])
+                    best = jnp.minimum(best, pair + float(apart * apart))
+                code[field, c, z] = encode(best)
+                after.append((cost, away))
+            return tuple(after)
+
+        lax.fori_loop(0, depth, settle, ((wall, nothing), (wall, nothing)), unroll=4)
+        for step in range(1, members):
+            send(c, step).start()
+        for copy in keep(c):
+            copy.start()
+
+    over_chunks(pass_chunk)
+
+    def finish(c):
+        hand_over(c).wait_send()
+        for copy in keep(c):
+            copy.wait()
+        for step in range(1, members):
+            send(c, step).wait()
+
+    over_chunks(finish)
+
+
+def depth_pass(seed_cost, occupied, unknown, half, members):
     robots, depth, _, lanes = seed_cost.shape
     rows = 16
-    steps = half // rows
+    chunks = half // rows
     reach = math.isqrt(int(largest_cost)) + 1
-    place = (lax.axis_index("robot") * steps).astype(jnp.int32).reshape(1)
-    shape = jax.ShapeDtypeStruct((depth, half, lanes), jnp.int16)
-    own = pl.BlockSpec((depth, rows, lanes), lambda i, p: (0, p[0] + i, 0))
-    here = pl.BlockSpec((depth, rows, lanes), lambda i, p: (0, i, 0))
+    anywhere = pl.BlockSpec(memory_space=pl.ANY)
+    copies = pltpu.SemaphoreType.DMA
     return pl.pallas_call(
         depth_kernel,
-        out_shape=(shape, shape),
-        grid_spec=pltpu.PrefetchScalarGridSpec(
-            num_scalar_prefetch=1,
-            grid=(steps,),
-            in_specs=[pl.BlockSpec((robots, depth, rows, lanes), lambda i, p: (0, 0, p[0] + i, 0)), here, own, own],
-            out_specs=(here, here),
-            scratch_shapes=[
-                pltpu.VMEM((2, depth + 2 * reach, rows, lanes), jnp.float32),
-                pltpu.VMEM((2, depth, rows, lanes), jnp.float32),
-            ],
+        out_shape=(
+            jax.ShapeDtypeStruct((members, depth // members, half, lanes), jnp.int16),
+            jax.ShapeDtypeStruct((depth, half, lanes), jnp.int16),
         ),
-        compiler_params=pltpu.CompilerParams(vmem_limit_bytes=56 * 2**20),
+        in_specs=[anywhere] * 3,
+        out_specs=(anywhere, anywhere),
+        scratch_shapes=[
+            pltpu.VMEM((chunks, robots, depth, rows, lanes), jnp.bfloat16),
+            pltpu.VMEM((chunks, robots, depth, rows, lanes), jnp.bfloat16),
+            pltpu.VMEM((chunks, depth, rows, lanes), jnp.int32),
+            pltpu.VMEM((chunks, depth, rows, lanes), jnp.int32),
+            pltpu.VMEM((chunks, depth, rows, lanes), jnp.bfloat16),
+            pltpu.VMEM((chunks, depth, rows, lanes), jnp.bfloat16),
+            pltpu.VMEM((2, chunks, depth, rows, lanes), jnp.int16),
+            pltpu.VMEM((2, depth + 2 * reach, rows, lanes), jnp.float32),
+            pltpu.VMEM((2, depth, rows, lanes), jnp.float32),
+            copies((chunks,)),
+            copies((3, chunks)),
+            copies((chunks,)),
+            copies((chunks,)),
+            copies((chunks, members - 1)),
+            copies((chunks, members - 1)),
+            copies((2, chunks)),
+        ],
+        compiler_params=pltpu.CompilerParams(vmem_limit_bytes=56 * 2**20, collective_id=0, has_side_effects=True),
         name="depth_pass",
-    )(place, seed_cost, other, occupied, unknown)
+    )(seed_cost, occupied, unknown)
 
 
 def envelope(f_ref, h_ref, low_ref, top_ref, bits_ref, reach_ref, near_ref, list_ref, extent, tile):
@@ -196,9 +303,16 @@
                 shift //= 2
             for r in range(8):
                 mask = joined[r, 0]
-                for j in range(word * 32, min(blocks, word * 32 + 32)):
-                    list_ref[count] = (group * 8 + r) * 1024 + j
-                    count = count + (lax.shift_right_logical(mask, j % 32) & 1)
+                for first in range(word * 32, min(blocks, word * 32 + 32), 8):
+                    some = lax.shift_right_logical(mask, first % 32) & 255
+
+                    def enlist(count, some=some, first=first, b=group * 8 + r):
+                        for j in range(8):
+                            list_ref[count] = b * 1024 + (first + j)
+                            count = count + (lax.shift_right_logical(some, j) & 1)
+                        return count
+
+                    count = lax.cond(some != 0, enlist, lambda count: count, count)
         return count
 
     count = lax.fori_loop(0, blocks // 8, bound, jnp.int32(0))
@@ -320,14 +434,13 @@
     depth, rows, lanes = occupied.shape
     half = rows // robots
     tile = depth // (robots * groups)
-    me = lax.axis_index("robot")
-    for_other = jnp.min(lax.dynamic_slice_in_dim(seed_cost, (1 - me) * half, half, 2), axis=0)
-    other = lax.ppermute(for_other, "robot", [(0, 1), (1, 0)])
-    fields = depth_pass(seed_cost, other, occupied, unknown, half)
+    members = robots * groups
+    out_received, in_codes = depth_pass(seed_cost, occupied, unknown, half, members)
+    in_received = lax.all_to_all(
+        in_codes.reshape(members, tile, half, lanes), ("robot", "xy"), split_axis=0, concat_axis=0, tiled=True
+    )
     settled = []
-    for field, label in zip(fields, ("out", "in")):
-        sent = field.reshape(robots * groups, tile, half, lanes)
-        received = lax.all_to_all(sent, ("robot", "xy"), split_axis=0, concat_axis=0, tiled=True)
+    for received, label in ((out_received, "out"), (in_received, "in")):
         crossed = row_pass(received, robots, strips, "row_pass_" + label)
         received = lax.all_to_all(crossed, "yz", split_axis=0, concat_axis=0, tiled=True)
         settled = [column_pass(received, "column_pass_" + label, *settled)]

time: 154 us -> 130 us (0.84); the launches traced: 152 us -> 131 us
  Pallas kernels: 73.8 us -> 108 us
  blocking collectives: 31.9 us -> 0 us
  waiting for transfers between devices: 28.7 us -> 8.68 us
  other arithmetic: 2.03 us -> 0 us
    pallas_call x1, Pallas kernels: 9.46 us -> 43.8 us  [depth_pass(): pl.pallas_call(depth_kernel, out_shape=(jax.ShapeDtypeStruct((members, de...]
    all_to_all x1 -> x0, blocking collectives: 31.9 us -> none  [fast_body(): lax.all_to_all(sent, ('robot', 'xy'), split_axis=0, concat_axis=0, tiled=...]
    ppermute x1 -> x0, waiting for transfers between devices: 23.2 us -> none  [fast_body(): other = lax.ppermute(for_other, 'robot', [(0, 1), (1, 0)])]
    ppermute x1 -> x0, starting transfers between devices: 3 us -> none  [fast_body(): other = lax.ppermute(for_other, 'robot', [(0, 1), (1, 0)])]
    all_to_all x1, starting transfers between devices: 3.56 us -> 6.14 us  [fast_body(): lax.all_to_all(in_codes.reshape(members, tile, half, lanes), ('robot', 'x...]
    reduce_min x1 -> x0, other arithmetic: 2.03 us -> none  [fast_body(): jnp.min(lax.dynamic_slice_in_dim(seed_cost, (1 - me) * half, half, 2), ax...]
    all_to_all x1, waiting for transfers between devices: 4.93 us -> 6.9 us  [fast_body(): lax.all_to_all(in_codes.reshape(members, tile, half, lanes), ('robot', 'x...]
  transfers between devices with their start and end apart: 4 -> 3, of which waited for: 3 -> 2; matrix products, arithmetic and copies ran while one was open for 0% -> 0% of each run, Pallas kernels for 33% -> 39%
where the time goes in v3:
time: 130 us; the launch traced here: 131 us
  Pallas kernels  108 us (83%)
  starting transfers between devices  13.2 us (10%)
  waiting for transfers between devices  8.68 us (7%)
    pallas_call x4, Pallas kernels, whole_call(): pl.pallas_call(kernel, out_shape=shape, in_specs=[vmem] * len(operands),...  64.2 us
    pallas_call x1, Pallas kernels, depth_pass(): pl.pallas_call(depth_kernel, out_shape=(jax.ShapeDtypeStruct((members, de...  43.8 us
    all_to_all x2, starting transfers between devices, fast_body(): lax.all_to_all(crossed, 'yz', split_axis=0, concat_axis=0, tiled=True)  7.03 us
    all_to_all x1, waiting for transfers between devices, fast_body(): lax.all_to_all(in_codes.reshape(members, tile, half, lanes), ('robot', 'x...  6.9 us
    all_to_all x1, starting transfers between devices, fast_body(): lax.all_to_all(in_codes.reshape(members, tile, half, lanes), ('robot', 'x...  6.14 us
  transfers between devices with their start and end apart: 3, of which 2 were waited for; matrix products, arithmetic and copies ran while one was open for 0% of the time, Pallas kernels for 39%

profile of v3, /device:TPU:0, one launch (start us, length us, event | category | flops | bytes accessed | tf_op | source)
XLA Modules:
  0.0 130.9 jit_solution(78411476769880706)
XLA Ops:
  0.0 43.8 %depth_pass.1 = (s16[8,8,64,128]{3,2,1,0:T(8,128)(2,1)}, s16[64,64,128]{2,1,0:T(8,128)(2,1)}) custom-call(bf16[2,64,128,128]{3,2,1,0:T(8,128)(2,1)} %cost_ref.1, s32[64,128,128]{2,1,0:T(8,128)} %occupied_ref.1, s32[64,128,128]{2,1,0:T(8,128)} %unknown_ref.1), custom_call_target="tpu_custom_call" | custom-call | tf_op jit(solution)/shard_map/depth_pass/pallas_call | solution.py:217
  43.8 6.1 %all-to-all-start = ((s16[8,8,64,128]{3,2,1,0:T(8,128)(2,1)}), s16[8,8,64,128]{3,2,1,0:T(8,128)(2,1)S(1)}, u32[]{:S(2)}, u32[]{:S(2)}) async-start(s16[8,8,64,128]{3,2,1,0:T(8,128)(2,1)} %bitcast.1), calls=%async_computation | async-start | bytes 2097152 | tf_op jit(solution)/shard_map/all_to_all | solution.py:439
  50.0 16.4 %row_pass_out.1 = s16[4,8,128,128]{3,2,1,0:T(8,128)(2,1)} custom-call(s16[8,8,64,128]{3,2,1,0:T(8,128)(2,1)} %get-tuple-element.8.in_ref), custom_call_target="tpu_custom_call" | custom-call | tf_op jit(solution)/shard_map/row_pass_out/pallas_call | solution.py:406
  66.4 6.9 %all-to-all-done.in_ref = s16[8,8,64,128]{3,2,1,0:T(8,128)(2,1)S(1)} async-done(((s16[8,8,64,128]{3,2,1,0:T(8,128)(2,1)}), s16[8,8,64,128]{3,2,1,0:T(8,128)(2,1)S(1)}, u32[]{:S(2)}, u32[]{:S(2)}) %all-to-all-start) | async-done | bytes 1048608 | tf_op jit(solution)/shard_map/all_to_all | solution.py:439
  73.3 0.0 copy-start.2
  73.3 3.5 %all-to-all-start.2 = ((s16[4,8,128,128]{3,2,1,0:T(8,128)(2,1)}), s16[4,8,128,128]{3,2,1,0:T(8,128)(2,1)S(1)}, u32[]{:S(2)}, u32[]{:S(2)}) async-start(s16[4,8,128,128]{3,2,1,0:T(8,128)(2,1)} %row_pass_out.1), calls=%async_computation.2 | async-start | bytes 2097152 | tf_op jit(solution)/shard_map/all_to_all | solution.py:445
  76.8 0.0 copy-done.2
  76.8 12.6 %row_pass_in.1 = s16[4,8,128,128]{3,2,1,0:T(8,128)(2,1)} custom-call(s16[8,8,64,128]{3,2,1,0:T(8,128)(2,1)} %copy-done.2), custom_call_target="tpu_custom_call" | custom-call | tf_op jit(solution)/shard_map/row_pass_in/pallas_call | solution.py:406
  89.5 1.8 %all-to-all-done.2.in_ref = s16[4,8,128,128]{3,2,1,0:T(8,128)(2,1)S(1)} async-done(((s16[4,8,128,128]{3,2,1,0:T(8,128)(2,1)}), s16[4,8,128,128]{3,2,1,0:T(8,128)(2,1)S(1)}, u32[]{:S(2)}, u32[]{:S(2)}) %all-to-all-start.2) | async-done | bytes 1048608 | tf_op jit(solution)/shard_map/all_to_all | solution.py:445
  91.3 0.0 copy-start
  91.3 3.5 %all-to-all-start.1 = ((s16[4,8,128,128]{3,2,1,0:T(8,128)(2,1)}), s16[4,8,128,128]{3,2,1,0:T(8,128)(2,1)S(1)}, u32[]{:S(2)}, u32[]{:S(2)}) async-start(s16[4,8,128,128]{3,2,1,0:T(8,128)(2,1)} %row_pass_in.1), calls=%async_computation.1 | async-start | bytes 2097152 | tf_op jit(solution)/shard_map/all_to_all | solution.py:445
  94.8 0.0 copy-done
  94.8 21.7 %column_pass_out.1.refs_0_ = f32[8,128,512]{2,1,0:T(8,128)} custom-call(s16[4,8,128,128]{3,2,1,0:T(8,128)(2,1)} %copy-done), custom_call_target="tpu_custom_call" | custom-call | tf_op jit(solution)/shard_map/column_pass_out/pallas_call | solution.py:406
  116.5 0.0 all-to-all-done.1.in_ref
  116.5 0.0 copy-start.1
  116.5 1.0 copy-done.1
  117.5 13.4 %column_pass_in.1 = f32[8,128,512]{2,1,0:T(8,128)} custom-call(s16[4,8,128,128]{3,2,1,0:T(8,128)(2,1)} %copy-done.1, f32[8,128,512]{2,1,0:T(8,128)} %column_pass_out.1.refs_0_), custom_call_target="tpu_custom_call" | custom-call | tf_op jit(solution)/shard_map/column_pass_in/pallas_call | solution.py:406
Async XLA Ops:
  43.8 29.5 %all-to-all-start = ((s16[8,8,64,128]{3,2,1,0:T(8,128)(2,1)}), s16[8,8,64,128]{3,2,1,0:T(8,128)(2,1)S(1)}, u32[]{:S(2)}, u32[]{:S(2)}) async-start(s16[8,8,64,128]{3,2,1,0:T(8,128)(2,1)} %bitcast.1), calls=%async_computation | async-start | bytes 2097152 | tf_op jit(solution)/shard_map/all_to_all | solution.py:439
  73.3 3.5 %copy-start.2 = (s16[8,8,64,128]{3,2,1,0:T(8,128)(2,1)}, s16[8,8,64,128]{3,2,1,0:T(8,128)(2,1)S(1)}, u32[]{:S(2)}) copy-start(s16[8,8,64,128]{3,2,1,0:T(8,128)(2,1)S(1)} %all-to-all-done.in_ref) | copy-start | bytes 3145732
  73.3 18.0 %all-to-all-start.2 = ((s16[4,8,128,128]{3,2,1,0:T(8,128)(2,1)}), s16[4,8,128,128]{3,2,1,0:T(8,128)(2,1)S(1)}, u32[]{:S(2)}, u32[]{:S(2)}) async-start(s16[4,8,128,128]{3,2,1,0:T(8,128)(2,1)} %row_pass_out.1), calls=%async_computation.2 | async-start | bytes 2097152 | tf_op jit(solution)/shard_map/all_to_all | solution.py:445
  91.3 3.5 %copy-start = (s16[4,8,128,128]{3,2,1,0:T(8,128)(2,1)}, s16[4,8,128,128]{3,2,1,0:T(8,128)(2,1)S(1)}, u32[]{:S(2)}) copy-start(s16[4,8,128,128]{3,2,1,0:T(8,128)(2,1)S(1)} %all-to-all-done.2.in_ref) | copy-start | bytes 3145732
  91.3 25.3 %all-to-all-start.1 = ((s16[4,8,128,128]{3,2,1,0:T(8,128)(2,1)}), s16[4,8,128,128]{3,2,1,0:T(8,128)(2,1)S(1)}, u32[]{:S(2)}, u32[]{:S(2)}) async-start(s16[4,8,128,128]{3,2,1,0:T(8,128)(2,1)} %row_pass_in.1), calls=%async_computation.1 | async-start | bytes 2097152 | tf_op jit(solution)/shard_map/all_to_all | solution.py:445
  116.5 1.0 copy-start.1
